TPU v7x, 32 devices: a whole 2x2x4 slice. The times are simulated.
32 devices in a mesh: section: 4 (over y, core), shard: 8 (over z, x).
Axes of the slice: x: 2, y: 2, z: 4, core: 2. Of those that a mesh axis runs over, the one named last changes fastest.
Arguments:
- train_weights: float32 [4, 16384, 1024], P('section', 'shard'), may hold values from -0.046875 to 0.046875
- section_to_group: int32 [4], replicated, may hold values from 0 to 3, each once
- hidden: bfloat16 [512, 16384], P(('section', 'shard')), may hold values from -6 to 6
- queries: bfloat16 [2048, 2048], P(('section', 'shard')), may hold values from -100 to 100
- kv_cache: bfloat16 [2048, 128, 256], P(('section', 'shard')), may hold values from -5 to 5
- lengths: int32 [512], P('section'), may hold values from 2 to 127, as said below
Outputs:
- context: bfloat16 [2048, 2048], P(('section', 'shard'))
- layer_out: bfloat16 [4, 4, 256, 16384], P('section', None, 'shard')
Inputs may be any that keep to these rules, and one draw needn't show every extreme that they name: `section_to_group`: a permutation: each rollout group runs exactly one trainer section's layer. `lengths`: every row has at least two cached tokens; some row of every device has 127.
All inputs are finite; a program needn't handle non-finite values.
Results may differ from a plain program's by a relative error of at most 0.006.
Values may be sent and summed in bfloat16 or wider, within the bound.
A program may use at most 64 MiB of HBM per device.

v0:
```python
import math

import jax
import jax.numpy as jnp
from jax import lax
from jax.sharding import PartitionSpec as P

D = 16384
HD = 128
QPK = 16
KVH = 4
LEN = 128
ROWS = 128


def route(blocks, source):
    spread = lax.all_to_all(blocks, "section", split_axis=2, concat_axis=0, tiled=True)
    picked = jnp.take(spread, source, axis=0)
    return lax.all_to_all(picked, "section", split_axis=0, concat_axis=2, tiled=True)


def attend(query_rows, cache_rows, fresh_rows, row_lengths):
    score_scale = 1.0 / math.sqrt(HD)
    cached_keys = cache_rows[:, :, :HD]
    cached_values = cache_rows[:, :, HD:]
    key_new = fresh_rows[:, :HD]
    value_new = fresh_rows[:, HD:]
    scores = (
        jnp.einsum("rhd,rtd->rht", query_rows, cached_keys, preferred_element_type=jnp.float32)
        * score_scale
    )
    valid = jnp.arange(LEN)[None, None, :] < row_lengths[:, None, None]
    scores = jnp.where(valid, scores, -1e30)
    fresh_score = (
        jnp.einsum("rhd,rd->rh", query_rows, key_new, preferred_element_type=jnp.float32)
        * score_scale
    )
    highest = jnp.maximum(jnp.max(scores, axis=-1), fresh_score)
    weights = jnp.where(valid, jnp.exp(scores - highest[..., None]), 0.0)
    fresh_weight = jnp.exp(fresh_score - highest)
    total = jnp.sum(weights, axis=-1) + fresh_weight
    probs = (weights / total[..., None]).astype(jnp.bfloat16)
    fresh_prob = (fresh_weight / total).astype(jnp.bfloat16)
    context = jnp.einsum("rht,rtd->rhd", probs, cached_values, preferred_element_type=jnp.float32)
    context = (
        context
        + fresh_prob.astype(jnp.float32)[..., None] * value_new.astype(jnp.float32)[:, None, :]
    )
    return context.reshape(context.shape[0], QPK * HD).astype(jnp.bfloat16)


def body(train_weights, section_to_group, hidden, queries, kv_cache, lengths):
    shards = lax.axis_size("shard")
    per_head = shards // KVH
    row_block = ROWS // per_head
    piece_cols = 2 * HD // shards
    source = jnp.argsort(section_to_group)
    flipped = train_weights[0].astype(jnp.bfloat16).T
    slice_rows = flipped.shape[1]
    routed = route(flipped[None], source)[0]
    pieces = routed.reshape(KVH, shards, piece_cols, slice_rows).transpose(1, 0, 2, 3)
    column_block = lax.all_to_all(pieces, "shard", split_axis=0, concat_axis=3, tiled=True)
    column_block = column_block.reshape(KVH * piece_cols, D)
    feature_block = lax.all_to_all(hidden, "shard", split_axis=1, concat_axis=0, tiled=True)
    partial_value = lax.dot_general(
        feature_block, routed, (((1,), (1,)), ((), ())), preferred_element_type=jnp.float32
    )
    arranged = partial_value.reshape(per_head, row_block, KVH, 2 * HD).transpose(2, 0, 1, 3)
    arranged = arranged.reshape(shards * row_block, 2 * HD)
    fresh = lax.psum_scatter(arranged, "shard", scatter_dimension=0, tiled=True).astype(
        jnp.bfloat16
    )
    position = lax.axis_index("shard")
    block_index = position % per_head
    row_lengths = lax.dynamic_slice_in_dim(lengths, block_index * row_block, row_block, 0)
    query_rows = queries.reshape(row_block, QPK, HD)
    context = attend(query_rows, kv_cache, fresh, row_lengths)
    layer_out = column_block.reshape(1, KVH, piece_cols, D)
    return (context, layer_out)


def solution(mesh):
    return jax.shard_map(
        body,
        mesh=mesh,
        in_specs=(
            P("section", "shard", None),
            P(),
            P(("section", "shard"), None),
            P(("section", "shard"), None),
            P(("section", "shard"), None, None),
            P("section"),
        ),
        out_specs=(P(("section", "shard"), None), P("section", None, "shard", None)),
        check_vma=False,
    )
```

profile of v0, /device:TPU:0, one launch (start us, length us, event | category | flops | bytes accessed | tf_op | source)
XLA Modules:
  0.0 370.3 jit_solution(17809616567040910189)
XLA Ops:
  7.2 7.3 %copy.30 = bf16[1,2048,1024]{1,2,0:T(8,128)(2,1)} copy(f32[1,2048,1024]{2,1,0:T(8,128)} %param.6) | data formatting | bytes 12582912 | tf_op args[0]
  14.4 20.6 %copy.31 = bf16[1,1024,2048]{1,0,2:T(2,128)(2,1)} copy(bf16[1,1024,2048]{2,1,0:T(8,128)(2,1)} %bitcast.51) | data formatting | bytes 8388608 | tf_op jit(solution)/shard_map/broadcast_in_dim | solution.py:60
  35.0 0.5 broadcast.33
  35.5 26.0 %reduce = bf16[2048,1024]{1,0:T(8,128)(2,1)} reduce(bf16[2048,1,1024]{2,1,0:T(2,128)(2,1)} %bitcast.48, bf16[]{:T(256)} %broadcast.33), dimensions={1}, to_apply=%bitcast.40.reduce_sub_computation | reduce | bytes 8388610
  61.5 6.2 %reshape.65 = bf16[4,2,262144]{2,1,0:T(2,128)(2,1)} reshape(bf16[2048,1024]{1,0:T(8,128)(2,1)} %reduce) | data formatting | bytes 8388608
  67.7 0.0 copy-start.2
  67.7 5.1 %all-to-all-start = ((bf16[4,2,262144]{2,1,0:T(2,128)(2,1)}), bf16[4,2,262144]{2,1,0:T(2,128)(2,1)}, u32[]{:S(2)}, u32[]{:S(2)}) async-start(bf16[4,2,262144]{2,1,0:T(2,128)(2,1)} %reshape.65), calls=%async_computation | async-start | bytes 8388608 | tf_op jit(solution)/shard_map/all_to_all | solution.py:17
  72.8 0.0 copy-done.2
  72.8 0.7 sort.17
  73.6 48.0 %all-to-all-done = bf16[4,2,262144]{2,1,0:T(2,128)(2,1)} async-done(((bf16[4,2,262144]{2,1,0:T(2,128)(2,1)}), bf16[4,2,262144]{2,1,0:T(2,128)(2,1)}, u32[]{:S(2)}, u32[]{:S(2)}) %all-to-all-start) | async-done | bytes 4194336 | tf_op jit(solution)/shard_map/all_to_all | solution.py:17
  121.6 7.4 %reshape.66 = bf16[2048,1,1024]{2,1,0:T(2,128)(2,1)} reshape(bf16[4,2,262144]{2,1,0:T(2,128)(2,1)} %all-to-all-done) | data formatting | bytes 8388608
  129.0 7.1 %copy.42 = bf16[1,1024,2048]{1,2,0:T(8,128)(2,1)} copy(bf16[1,1024,2048]{1,0,2:T(2,128)(2,1)} %bitcast.49) | data formatting | bytes 8388608
  136.1 6.2 %copy.32 = bf16[1,1024,4,512]{3,1,2,0:T(8,128)(2,1)} copy(bf16[1,1024,4,512]{1,3,2,0:T(8,128)(2,1)} %bitcast.52) | data formatting | bytes 8388608 | tf_op jit(solution)/shard_map/all_to_all | solution.py:17
  142.3 5.0 %gather_fusion = bf16[4,1024,512]{2,1,0:T(8,128)(2,1)} fusion(bf16[4,1024,512]{2,1,0:T(8,128)(2,1)} %bitcast.53, s32[1024]{0:T(1024)S(1)} %pad_clamp_fusion), kind=kCustom, calls=%fused_computation | custom fusion | bytes 8388624 | tf_op jit(solution)/shard_map/jit(_take)/gather | solution.py:18
  147.3 4.7 %broadcast_select_fusion = bf16[4,1024,512]{2,1,0:T(8,128)(2,1)} fusion(bf16[4,1024,512]{2,1,0:T(8,128)(2,1)} %gather_fusion, pred[4]{0:T(512)(128)(4,1)S(1)} %compare_and_fusion), kind=kLoop, calls=%fused_computation.2 | loop fusion | flops 2097152 | bytes 8388612 | tf_op jit(solution)/shard_map/jit(_take)/select_n | solution.py:18
  152.0 0.0 copy-start
  152.0 5.0 %all-to-all-start.1 = ((bf16[4,1024,512]{2,1,0:T(8,128)(2,1)}), bf16[4,1024,512]{2,1,0:T(8,128)(2,1)}, u32[]{:S(2)}, u32[]{:S(2)}) async-start(bf16[4,1024,512]{2,1,0:T(8,128)(2,1)} %broadcast_select_fusion), calls=%async_computation.1 | async-start | bytes 8388608 | tf_op jit(solution)/shard_map/all_to_all | solution.py:19
  157.0 0.0 copy-done
  157.0 0.9 copy.51
  157.8 47.4 %all-to-all-done.1 = bf16[4,1024,512]{2,1,0:T(8,128)(2,1)} async-done(((bf16[4,1024,512]{2,1,0:T(8,128)(2,1)}), bf16[4,1024,512]{2,1,0:T(8,128)(2,1)}, u32[]{:S(2)}, u32[]{:S(2)}) %all-to-all-start.1) | async-done | bytes 4194336 | tf_op jit(solution)/shard_map/all_to_all | solution.py:19
  205.2 6.7 %all-to-all-start.2 = ((bf16[16,8,2048]{2,0,1:T(8,128)(2,1)}), bf16[16,8,2048]{2,0,1:T(8,128)(2,1)S(1)}, u32[]{:S(2)}, u32[]{:S(2)}) async-start(bf16[16,8,2048]{2,0,1:T(8,128)(2,1)} %bitcast.46), calls=%async_computation.2 | async-start | bytes 1048576 | tf_op jit(solution)/shard_map/all_to_all | solution.py:64
  211.9 7.4 %copy.37 = bf16[1,1024,4,512]{3,2,1,0:T(4,128)(2,1)} copy(bf16[1,1024,4,512]{3,1,2,0:T(8,128)(2,1)} %bitcast.6) | data formatting | bytes 8388608 | tf_op jit(solution)/shard_map/all_to_all | solution.py:19
  219.4 7.8 %reshape_squeeze.3 = bf16[4,8,32,2048]{3,2,1,0:T(8,128)(2,1)} reshape(bf16[1,1024,4,512]{3,2,1,0:T(4,128)(2,1)} %copy.37) | data formatting | bytes 8388608 | tf_op jit(solution)/shard_map/reshape;squeeze | solution.py:61
  227.2 4.7 %copy.38 = bf16[8,4,32,2048]{3,2,1,0:T(8,128)(2,1)} copy(bf16[8,4,32,2048]{3,2,0,1:T(8,128)(2,1)} %bitcast.54) | data formatting | bytes 8388608 | tf_op jit(solution)/shard_map/transpose | solution.py:61
  231.9 0.0 all-to-all-done.2
  231.9 6.0 %all-to-all-start.3 = ((bf16[8,4,32,2048]{3,2,1,0:T(8,128)(2,1)}), bf16[8,4,32,2048]{3,2,1,0:T(8,128)(2,1)}, u32[]{:S(2)}, u32[]{:S(2)}) async-start(bf16[8,4,32,2048]{3,2,1,0:T(8,128)(2,1)} %copy.38), calls=%async_computation.4 | async-start | bytes 8388608 | tf_op jit(solution)/shard_map/all_to_all | solution.py:62
  237.9 0.0 reduce-scatter.2.cloned.1.call-start
  238.0 6.2 %copy.33 = bf16[1,1024,4,512]{1,3,2,0:T(8,128)(2,1)} copy(bf16[1,1024,4,512]{3,1,2,0:T(8,128)(2,1)} %bitcast.6) | data formatting | bytes 8388608 | tf_op jit(solution)/shard_map/all_to_all | solution.py:19
  244.2 0.0 copy-start.1
  244.2 0.0 copy-start.3
  244.2 3.5 convolution_bitcast_fusion
  247.7 0.2 copy.35
  247.9 0.2 reshape.52
  248.1 0.9 copy.36
  249.0 0.0 reduce-scatter.2.cloned.1.call-update
  249.1 0.0 copy-done.1
  249.1 0.0 copy-done.3
  249.1 0.1 dynamic_slice.3
  249.2 0.1 iota_compare_fusion
  249.3 2.9 fusion.26
  252.2 101.9 %reduce-scatter.2.cloned.1.call-done = f32[64,256]{1,0:T(8,128)} async-done(((f32[512,256]{1,0:T(8,128)}), f32[64,256]{1,0:T(8,128)}) %reduce-scatter.2.cloned.1.call-update) | async-done | bytes 65552 | tf_op jit(solution)/shard_map/reduce_scatter | solution.py:70
  354.1 0.8 convert_element_type.29
  354.9 0.2 fusion.21
  355.2 0.4 fusion.16
  355.6 2.3 fusion.13
  357.9 0.8 copy.52
  358.7 0.0 all-to-all-done.3
  358.7 4.8 %copy.44 = bf16[1,8,4,4,8,2048]{5,4,1,3,2,0:T(8,128)(2,1)} copy(bf16[1,8,4,4,8,2048]{5,4,3,2,1,0:T(8,128)(2,1)} %bitcast.28) | data formatting | bytes 8388608 | tf_op jit(solution)/shard_map/all_to_all | solution.py:62
  (8 shorter events, 0.1 us)
Async XLA Ops:
  67.7 5.1 %copy-start.2 = (s32[4]{0:T(128)S(1)}, s32[4]{0:T(128)}, u32[]{:S(2)}) copy-start(s32[4]{0:T(128)} %param.7) | copy-start | bytes 52
  67.7 53.8 %all-to-all-start = ((bf16[4,2,262144]{2,1,0:T(2,128)(2,1)}), bf16[4,2,262144]{2,1,0:T(2,128)(2,1)}, u32[]{:S(2)}, u32[]{:S(2)}) async-start(bf16[4,2,262144]{2,1,0:T(2,128)(2,1)} %reshape.65), calls=%async_computation | async-start | bytes 8388608 | tf_op jit(solution)/shard_map/all_to_all | solution.py:17
  152.0 5.0 %copy-start = (bf16[16,16384]{1,0:T(8,128)(2,1)S(1)}, bf16[16,16384]{1,0:T(8,128)(2,1)}, u32[]{:S(2)}) copy-start(bf16[16,16384]{1,0:T(8,128)(2,1)} %param.8) | copy-start | bytes 1572868
  152.0 53.2 %all-to-all-start.1 = ((bf16[4,1024,512]{2,1,0:T(8,128)(2,1)}), bf16[4,1024,512]{2,1,0:T(8,128)(2,1)}, u32[]{:S(2)}, u32[]{:S(2)}) async-start(bf16[4,1024,512]{2,1,0:T(8,128)(2,1)} %broadcast_select_fusion), calls=%async_computation.1 | async-start | bytes 8388608 | tf_op jit(solution)/shard_map/all_to_all | solution.py:19
  205.2 26.7 %all-to-all-start.2 = ((bf16[16,8,2048]{2,0,1:T(8,128)(2,1)}), bf16[16,8,2048]{2,0,1:T(8,128)(2,1)S(1)}, u32[]{:S(2)}, u32[]{:S(2)}) async-start(bf16[16,8,2048]{2,0,1:T(8,128)(2,1)} %bitcast.46), calls=%async_computation.2 | async-start | bytes 1048576 | tf_op jit(solution)/shard_map/all_to_all | solution.py:64
  231.9 126.8 %all-to-all-start.3 = ((bf16[8,4,32,2048]{3,2,1,0:T(8,128)(2,1)}), bf16[8,4,32,2048]{3,2,1,0:T(8,128)(2,1)}, u32[]{:S(2)}, u32[]{:S(2)}) async-start(bf16[8,4,32,2048]{3,2,1,0:T(8,128)(2,1)} %copy.38), calls=%async_computation.4 | async-start | bytes 8388608 | tf_op jit(solution)/shard_map/all_to_all | solution.py:62
  237.9 116.1 %reduce-scatter.2.cloned.1.call-start = ((), (), s32[]{:S(2)}) async-start(), calls=%async_computation.5 | async-start | bytes 589824 | tf_op jit(solution)/shard_map/reduce_scatter | solution.py:70
  244.2 4.9 %copy-start.1 = (bf16[64,2048]{1,0:T(8,128)(2,1)S(1)}, bf16[64,2048]{1,0:T(8,128)(2,1)}, u32[]{:S(2)}) copy-start(bf16[64,2048]{1,0:T(8,128)(2,1)} %param.9) | copy-start | bytes 786436
  244.2 5.0 %copy-start.3 = (s32[128]{0:T(128)S(1)}, s32[128]{0:T(128)}, u32[]{:S(2)}) copy-start(s32[128]{0:T(128)} %param.11) | copy-start | bytes 1540
Sparse Core Ops, SparseCore 0:
  249.2 104.8 reduce-scatter.1
where the time goes:
time: 372 us; the launch traced here: 370 us
  waiting for transfers between devices  197 us (53%)
  local copies, waits for them, and re-layouts  94.4 us (25%)
  other arithmetic  32.8 us (9%)
  starting transfers between devices  22.8 us (6%)
  between operations  14.2 us (4%)
  matrix products  8.94 us (2%)
    reduce_scatter x1, waiting for transfers between devices, body(): lax.psum_scatter(arranged, 'shard', scatter_dimension=0, tiled=True)  102 us
    all_to_all x1, waiting for transfers between devices, route(): lax.all_to_all(blocks, 'section', split_axis=2, concat_axis=0, tiled=True)  48 us
    all_to_all x1, waiting for transfers between devices, route(): lax.all_to_all(picked, 'section', split_axis=0, concat_axis=2, tiled=True)  47.4 us
    unnamed x15, local copies, waits for them, and re-layouts  29.4 us
    unnamed x1, other arithmetic  26 us
    broadcast_in_dim x1, local copies, waits for them, and re-layouts, body(): routed = route(flipped[None], source)[0]  20.6 us
    all_to_all x2, local copies, waits for them, and re-layouts, route(): lax.all_to_all(picked, 'section', split_axis=0, concat_axis=2, tiled=True)  13.6 us
    another operation x1, local copies, waits for them, and re-layouts, body(): routed.reshape(KVH, shards, piece_cols, slice_rows).transpose(1, 0, 2, 3)  7.81 us
  transfers between devices with their start and end apart: 5, of which 3 were waited for; matrix products, arithmetic and copies ran while one was open for 11% of the time, Pallas kernels for 0%

commit v1 on v0

--- a/solution.py
+++ b/solution.py
@@ -1,8 +1,11 @@
+import functools
 import math
 
 import jax
 import jax.numpy as jnp
 from jax import lax
+from jax.experimental import pallas as pl
+from jax.experimental.pallas import tpu as pltpu
 from jax.sharding import PartitionSpec as P
 
 D = 16384
@@ -49,7 +52,7 @@
     return context.reshape(context.shape[0], QPK * HD).astype(jnp.bfloat16)
 
 
-def body(train_weights, section_to_group, hidden, queries, kv_cache, lengths):
+def plain_body(train_weights, section_to_group, hidden, queries, kv_cache, lengths):
     shards = lax.axis_size("shard")
     per_head = shards // KVH
     row_block = ROWS // per_head
@@ -79,7 +82,228 @@
     return (context, layer_out)
 
 
+def flip(index, mask, size):
+    result, bit = 0, 1
+    while bit < size:
+        value = (index // bit) % 2
+        if mask & bit:
+            value = 1 - value
+        result = result + value * bit
+        bit *= 2
+    return result
+
+
+def move_kernel(sections, shards, source_ref, w_ref, hidden_ref, out_ref, fresh_ref, *scratch):
+    spread = scratch[:shards]
+    (stage, picked, feat, part, part_send, part_recv,
+     a_send, a_recv, b_send, b_recv, c_send, c_recv, h_send, h_recv, p_send, p_recv, local) = scratch[shards:]
+    me = lax.axis_index("section")
+    pos = lax.axis_index("shard")
+    heads, _, piece, width = w_ref.shape
+    rows_in = hidden_ref.shape[0]
+    per_head = shards // heads
+    row_block = ROWS // per_head
+
+    barrier = pltpu.get_barrier_semaphore()
+    for j in range(1, sections):
+        pl.semaphore_signal(barrier, inc=1, device_id={"section": flip(me, j, sections)}, device_id_type=pl.DeviceIdType.MESH)
+    for j in range(1, shards):
+        pl.semaphore_signal(barrier, inc=1, device_id={"shard": flip(pos, j, shards)}, device_id_type=pl.DeviceIdType.MESH)
+    pl.semaphore_wait(barrier, sections + shards - 2)
+
+    def remote(src, dst, send, recv, **target):
+        return pltpu.make_async_remote_copy(
+            src_ref=src, dst_ref=dst, send_sem=send, recv_sem=recv,
+            device_id=target, device_id_type=pl.DeviceIdType.MESH)
+
+    masks = list(range(shards - 1, -1, -1))
+
+    def spread_copies(k):
+        p = flip(pos, masks[k], shards)
+        copies = []
+        for j in range(1, sections):
+            t = flip(me, j, sections)
+            copies.append(remote(w_ref.at[t, p], spread[k].at[me], a_send.at[k, j], a_recv.at[k, j], section=t))
+        return copies
+
+    def collect_copies(k):
+        copies = []
+        for j in range(1, sections):
+            t = flip(me, j, sections)
+            copies.append(remote(stage.at[k, t], picked.at[k, me], b_send.at[k, j], b_recv.at[k, j], section=t))
+        return copies
+
+    columns = pl.ds(pl.multiple_of(pos * width, width), width)
+
+    def keep_copy(k):
+        p = flip(pos, masks[k], shards)
+        if masks[k] == 0:
+            return pltpu.make_async_copy(picked.at[k], out_ref.at[:, :, columns], local)
+        return remote(picked.at[k], out_ref.at[:, :, columns], c_send.at[k], c_recv.at[k], shard=p)
+
+    def hidden_copy(j):
+        p = flip(pos, j, shards)
+        return remote(hidden_ref.at[:, pl.ds(pl.multiple_of(p * width, width), width)], feat.at[pos],
+                      h_send.at[j], h_recv.at[j], shard=p)
+
+    def start_spread(k):
+        for copy in spread_copies(k):
+            copy.start()
+        spread[k][me] = w_ref[me, flip(pos, masks[k], shards)]
+
+    ahead = AHEAD
+    for k in range(min(ahead, shards)):
+        start_spread(k)
+    for j in range(1, shards):
+        hidden_copy(j).start()
+    feat[pos] = hidden_ref[:, columns]
+
+    def collect(k):
+        for copy in spread_copies(k):
+            copy.wait()
+        for g in range(sections):
+            stage[k, g] = spread[k][source_ref[g]]
+        picked[k, me] = stage[k, me]
+        for copy in collect_copies(k):
+            copy.start()
+
+    def forward(k):
+        for copy in collect_copies(k):
+            copy.wait()
+        keep_copy(k).start()
+        if k == 0:
+            for j in range(1, shards):
+                hidden_copy(j).wait()
+        p = flip(pos, masks[k], shards)
+        value = lax.dot_general(
+            picked[k].reshape(heads * piece, width), feat[...].reshape(shards * rows_in, width),
+            (((1,), (1,)), ((), ())), preferred_element_type=jnp.float32)
+        for h in range(heads):
+            part[h, pl.ds(pl.multiple_of(p * piece, piece), piece), :] = value[h * piece:(h + 1) * piece]
+
+    for k in range(shards):
+        collect(k)
+        if k + ahead < shards:
+            start_spread(k + ahead)
+        if k >= 1:
+            forward(k - 1)
+    forward(shards - 1)
+
+    for h in range(heads):
+        turned = part[h].T
+        for b in range(per_head):
+            part_send[h * per_head + b] = turned[b * row_block:(b + 1) * row_block]
+
+    def part_copy(j):
+        p = flip(pos, j, shards)
+        return remote(part_send.at[p], part_recv.at[j], p_send.at[j], p_recv.at[j], shard=p)
+
+    for j in range(shards - 1, 0, -1):
+        part_copy(j).start()
+    total = part_send[pos]
+    for j in range(1, shards):
+        part_copy(j).wait()
+        total = total + part_recv[j]
+    fresh_ref[...] = total.astype(fresh_ref.dtype)
+    for k in range(shards):
+        keep_copy(k).wait()
+
+
+AHEAD = 3
+
+
+def move(weights, hidden, source):
+    sections, shards = lax.axis_size("section"), lax.axis_size("shard")
+    heads, _, piece, width = weights.shape
+    rows_in = hidden.shape[0]
+    row_block = ROWS * heads // shards
+    vmem = pl.BlockSpec(memory_space=pltpu.VMEM)
+    dma = pltpu.SemaphoreType.DMA
+    return pl.pallas_call(
+        functools.partial(move_kernel, sections, shards),
+        out_shape=(
+            jax.ShapeDtypeStruct((heads, piece, shards * width), jnp.bfloat16),
+            jax.ShapeDtypeStruct((row_block, 2 * HD), jnp.bfloat16),
+        ),
+        in_specs=[pl.BlockSpec(memory_space=pltpu.SMEM), vmem, vmem],
+        out_specs=(pl.BlockSpec(memory_space=pl.ANY), vmem),
+        scratch_shapes=[pltpu.VMEM((sections, piece, width), jnp.bfloat16)] * shards + [
+            pltpu.VMEM((shards, sections, piece, width), jnp.bfloat16),
+            pltpu.VMEM((shards, heads, piece, width), jnp.bfloat16),
+            pltpu.VMEM((shards, rows_in, width), jnp.bfloat16),
+            pltpu.VMEM((heads, 2 * HD, ROWS), jnp.float32),
+            pltpu.VMEM((shards, row_block, 2 * HD), jnp.float32),
+            pltpu.VMEM((shards, row_block, 2 * HD), jnp.float32),
+            dma((shards, sections)), dma((shards, sections)),
+            dma((shards, sections)), dma((shards, sections)),
+            dma((shards,)), dma((shards,)), dma((shards,)), dma((shards,)), dma((shards,)), dma((shards,)),
+            dma(()),
+        ],
+        compiler_params=pltpu.CompilerParams(
+            collective_id=0, has_side_effects=True, vmem_limit_bytes=40 * 2**20),
+        cost_estimate=pl.CostEstimate(flops=2 * ROWS * width * heads * piece * shards, bytes_accessed=4 * weights.size, transcendentals=0),
+    )(source, weights, hidden)
+
+
+def attend_kernel(query_ref, cache_ref, fresh_ref, length_ref, out_ref):
+    scale = 1.0 / math.sqrt(HD)
+    query = query_ref[...]
+    cache = cache_ref[...]
+    fresh = fresh_ref[...].astype(jnp.float32)
+    scores = lax.dot_general(query, cache[:, :, :HD], (((2,), (2,)), ((0,), (0,))),
+                             preferred_element_type=jnp.float32) * scale
+    slot = lax.broadcasted_iota(jnp.int32, scores.shape, 2)
+    valid = slot < length_ref[...]
+    scores = jnp.where(valid, scores, -1e30)
+    fresh_score = jnp.sum(query.astype(jnp.float32) * fresh[:, :, :HD], axis=-1, keepdims=True) * scale
+    highest = jnp.maximum(jnp.max(scores, axis=-1, keepdims=True), fresh_score)
+    weights = jnp.where(valid, jnp.exp(scores - highest), 0.0)
+    fresh_weight = jnp.exp(fresh_score - highest)
+    total = jnp.sum(weights, axis=-1, keepdims=True) + fresh_weight
+    probs = (weights / total).astype(jnp.bfloat16)
+    fresh_prob = (fresh_weight / total).astype(jnp.bfloat16).astype(jnp.float32)
+    context = lax.dot_general(probs, cache[:, :, HD:], (((2,), (1,)), ((0,), (0,))),
+                              preferred_element_type=jnp.float32)
+    context = context + fresh_prob * fresh[:, :, HD:]
+    out_ref[...] = context.astype(out_ref.dtype)
+
+
+def attend_rows(queries, cache, fresh, row_lengths):
+    entries = cache.shape[0]
+    step = 8
+    spec = lambda *tail: pl.BlockSpec((step,) + tail, lambda i: (i, 0, 0))
+    lengths = jnp.broadcast_to(row_lengths[:, None, None], (entries, 1, LEN))
+    return pl.pallas_call(
+        attend_kernel,
+        grid=(entries // step,),
+        out_shape=jax.ShapeDtypeStruct((entries, QPK, HD), jnp.bfloat16),
+        in_specs=[spec(QPK, HD), spec(LEN, 2 * HD), spec(1, 2 * HD), spec(1, LEN)],
+        out_specs=spec(QPK, HD),
+    )(queries.reshape(entries, QPK, HD), cache, fresh.reshape(entries, 1, 2 * HD), lengths).reshape(entries, QPK * HD)
+
+
+def chunk_body(train_weights, section_to_group, hidden, queries, kv_cache, lengths):
+    shards = lax.axis_size("shard")
+    per_head = shards // KVH
+    row_block = ROWS // per_head
+    piece = 2 * HD // shards
+    source = jnp.argsort(section_to_group).astype(jnp.int32)
+    flipped = train_weights[0].astype(jnp.bfloat16).T
+    weights = flipped.reshape(KVH, shards, piece, flipped.shape[1])
+    kept, fresh = move(weights, hidden, source)
+    block = lax.axis_index("shard") % per_head
+    row_lengths = lax.dynamic_slice_in_dim(lengths, block * row_block, row_block, 0)
+    context = attend_rows(queries, kv_cache, fresh, row_lengths)
+    return (context, kept[None])
+
+
 def solution(mesh):
+    sections, shards = mesh.shape["section"], mesh.shape["shard"]
+    chunked = (
+        sections == KVH and shards % KVH == 0 and shards & (shards - 1) == 0
+        and (2 * HD // shards) % 16 == 0 and (ROWS // shards) % 16 == 0
+    )
+    body = chunk_body if chunked else plain_body
     return jax.shard_map(
         body,
         mesh=mesh,

time: 372 us -> 180 us (0.48)
  waiting for transfers between devices: 197 us -> 0 us
  Pallas kernels: 0 us -> 152 us
  local copies, waits for them, and re-layouts: 94.4 us -> 19.9 us
  other arithmetic: 32.8 us -> 6.81 us
  starting transfers between devices: 22.8 us -> 0 us
  between operations: 14.2 us -> 0.67 us
  matrix products: 8.94 us -> 0 us
    pallas_call x0 -> x2, Pallas kernels: none -> 152 us  [the longest x1 144 us: move(): pl.pallas_call(functools.partial(move_kernel, sections, shards), out_shap...]
    reduce_scatter x1 -> x0, waiting for transfers between devices: 102 us -> none  [body(): lax.psum_scatter(arranged, 'shard', scatter_dimension=0, tiled=True)]
    all_to_all x4 -> x0, waiting for transfers between devices: 95.3 us -> none  [the longest x1 48 us: route(): lax.all_to_all(blocks, 'section', split_axis=2, concat_axis=0, tiled=True)]
    unnamed x1 -> x0, other arithmetic: 26 us -> none
    all_to_all x5 -> x0, local copies, waits for them, and re-layouts: 25.5 us -> none  [the longest x2 13.6 us: route(): lax.all_to_all(picked, 'section', split_axis=0, concat_axis=2, tiled=True)]
    all_to_all x4 -> x0, starting transfers between devices: 22.8 us -> none  [the longest x1 6.72 us: body(): lax.all_to_all(hidden, 'shard', split_axis=1, concat_axis=0, tiled=True)]
    broadcast_in_dim x1, local copies, waits for them, and re-layouts: 20.6 us -> 0.74 us  [attend_rows(): lengths = jnp.broadcast_to(row_lengths[:, None, None], (entries, 1, LEN))]
    unnamed x15 -> x13, local copies, waits for them, and re-layouts: 29.4 us -> 11.2 us
  transfers between devices with their start and end apart: 5 -> 0, of which waited for: 3 -> 0; matrix products, arithmetic and copies ran while one was open for 11% -> 0% of each run, Pallas kernels for 0% -> 0%
where the time goes in v1:
time: 180 us; the launch traced here: 179 us
  Pallas kernels  152 us (84%)
  local copies, waits for them, and re-layouts  19.9 us (11%)
  other arithmetic  6.81 us (4%)
    pallas_call x1, Pallas kernels, move(): pl.pallas_call(functools.partial(move_kernel, sections, shards), out_shap...  144 us
    unnamed x13, local copies, waits for them, and re-layouts  11.2 us
    pallas_call x1, Pallas kernels, attend_rows(): pl.pallas_call(attend_kernel, grid=(entries // step,), out_shape=jax.Shap...  7.71 us
    transpose x1, local copies, waits for them, and re-layouts, chunk_body(): flipped = train_weights[0].astype(jnp.bfloat16).T  6.57 us
    transpose x1, other arithmetic, chunk_body(): flipped = train_weights[0].astype(jnp.bfloat16).T  6.06 us

profile of v1, /device:TPU:0, one launch (start us, length us, event | category | flops | bytes accessed | tf_op | source)
XLA Modules:
  0.0 179.0 jit_solution(12771390187001451429)
XLA Ops:
  0.6 0.7 dynamic_slice.3
  1.4 0.7 broadcast_in_dim.4.length_ref
  2.1 6.1 %convert_bitcast_fusion = bf16[1024,2048]{0,1:T(8,128)(2,1)} fusion(f32[1,2048,1024]{2,1,0:T(8,128)} %param.6), kind=kLoop, calls=%fused_computation | loop fusion | flops 2097152 | bytes 12582912 | tf_op jit(solution)/shard_map/transpose | solution.py:291
  8.2 0.0 copy-start.4
  8.2 0.0 copy-start.2
  8.2 0.0 copy-start.3
  8.2 6.6 %copy.9 = bf16[1024,2048]{1,0:T(8,128)(2,1)} copy(bf16[1024,2048]{0,1:T(8,128)(2,1)} %convert_bitcast_fusion) | data formatting | bytes 8388608 | tf_op jit(solution)/shard_map/transpose | solution.py:291
  14.8 0.0 copy-done.4
  14.8 0.7 sort.17
  15.5 0.0 copy-done.2
  15.5 0.0 copy-start
  15.5 2.2 %copy-done = bf16[1024,2048]{1,0:T(8,128)(2,1)S(1)} copy-done((bf16[1024,2048]{1,0:T(8,128)(2,1)S(1)}, bf16[1024,2048]{1,0:T(8,128)(2,1)}, u32[]{:S(2)}) %copy-start) | copy-done | bytes 4194328
  17.7 144.0 %shard_map.77 = (bf16[4,32,16384]{2,1,0:T(8,128)(2,1)S(1)}, bf16[64,256]{1,0:T(8,128)(2,1)S(1)}) custom-call(s32[4]{0:T(128)S(1)} %get-tuple-element.5.source_ref, bf16[4,8,32,2048]{3,2,1,0:T(8,128)(2,1)S(1)} %bitcast.13, bf16[16,16384]{1,0:T(8,128)(2,1)S(1)} %copy-done.2), custom_call_target="tpu_custom_call" | custom-call | flops 536870912 | bytes 8388608 | tf_op jit(solution)/shard_map/pallas_call | solution.py:222
  161.7 0.0 copy-start.1
  161.7 1.9 %copy-done.1 = bf16[4,32,16384]{2,1,0:T(8,128)(2,1)} copy-done((bf16[4,32,16384]{2,1,0:T(8,128)(2,1)}, bf16[4,32,16384]{2,1,0:T(8,128)(2,1)S(1)}, u32[]{:S(2)}) %copy-start.1) | copy-done | bytes 4194328
  163.6 0.7 copy.10.fresh_ref
  164.3 0.0 copy-done.3
  164.3 0.7 copy.11
  165.0 7.7 %shard_map.78 = bf16[64,16,128]{2,1,0:T(8,128)(2,1)} custom-call(bf16[64,16,128]{2,1,0:T(8,128)(2,1)} %bitcast.17, bf16[64,128,256]{2,1,0:T(8,128)(2,1)} %cache_ref.1, bf16[64,1,256]{2,1,0:T(2,128)(2,1)} %copy.10.fresh_ref, s32[64,1,128]{2,1,0:T(1,128)} %broadcast_in_dim.4.length_ref), custom_call_target="tpu_custom_call" | custom-call | tf_op jit(solution)/shard_map/pallas_call | solution.py:276
  172.8 1.7 copy.14
  174.5 4.6 %copy.16 = bf16[1,4,32,16384]{3,2,1,0:T(8,128)(2,1)} copy(bf16[1,4,32,16384]{3,2,1,0:T(8,128)(2,1)} %bitcast.14) | data formatting | bytes 8388608
  (1 shorter events, 0.0 us)
Async XLA Ops:
  8.2 6.6 %copy-start.4 = (s32[4]{0:T(128)S(1)}, s32[4]{0:T(128)}, u32[]{:S(2)}) copy-start(s32[4]{0:T(128)} %param.7) | copy-start | bytes 52
  8.2 7.3 %copy-start.2 = (bf16[16,16384]{1,0:T(8,128)(2,1)S(1)}, bf16[16,16384]{1,0:T(8,128)(2,1)}, u32[]{:S(2)}) copy-start(bf16[16,16384]{1,0:T(8,128)(2,1)} %hidden_ref.1) | copy-start | bytes 1572868
  8.2 156.1 %copy-start.3 = (bf16[64,2048]{1,0:T(8,128)(2,1)S(1)}, bf16[64,2048]{1,0:T(8,128)(2,1)}, u32[]{:S(2)}) copy-start(bf16[64,2048]{1,0:T(8,128)(2,1)} %param.9) | copy-start | bytes 786436
  15.5 2.2 %copy-start = (bf16[1024,2048]{1,0:T(8,128)(2,1)S(1)}, bf16[1024,2048]{1,0:T(8,128)(2,1)}, u32[]{:S(2)}) copy-start(bf16[1024,2048]{1,0:T(8,128)(2,1)} %copy.9) | copy-start | bytes 12582916
  161.7 1.9 %copy-start.1 = (bf16[4,32,16384]{2,1,0:T(8,128)(2,1)}, bf16[4,32,16384]{2,1,0:T(8,128)(2,1)S(1)}, u32[]{:S(2)}) copy-start(bf16[4,32,16384]{2,1,0:T(8,128)(2,1)S(1)} %get-tuple-element.7) | copy-start | bytes 12582916

commit v2 on v1

--- a/solution.py
+++ b/solution.py
@@ -93,16 +93,36 @@
     return result
 
 
-def move_kernel(sections, shards, source_ref, w_ref, hidden_ref, out_ref, fresh_ref, *scratch):
+def move_kernel(sections, shards, source_ref, train_ref, hidden_ref, out_ref, fresh_ref, *scratch):
     spread = scratch[:shards]
     (stage, picked, feat, part, part_send, part_recv,
-     a_send, a_recv, b_send, b_recv, c_send, c_recv, h_send, h_recv, p_send, p_recv, local) = scratch[shards:]
+     a_send, a_recv, b_send, b_recv, c_send, c_recv, h_send, h_recv, p_send, p_recv, local, w_ref, raw, raw_sem) = scratch[shards:]
     me = lax.axis_index("section")
     pos = lax.axis_index("shard")
     heads, _, piece, width = w_ref.shape
     rows_in = hidden_ref.shape[0]
     per_head = shards // heads
     row_block = ROWS // per_head
+
+    lanes = raw.shape[-1]
+    together = lanes // piece
+    groups = shards // together
+
+    def group_of(i):
+        return flip(pos // together, groups - 1 - i, groups)
+
+    def load_copy(i, h):
+        start = pl.multiple_of((h * groups + group_of(i)) * lanes, lanes)
+        return pltpu.make_async_copy(train_ref.at[:, pl.ds(start, lanes)], raw.at[i, h], raw_sem.at[i, h])
+
+    def turn(i, h):
+        load_copy(i, h).wait()
+        block = raw[i, h].astype(jnp.bfloat16).T
+        w_ref[h, pl.ds(group_of(i) * together, together)] = block.reshape(together, piece, width)
+
+    for i in range(groups):
+        for h in range(heads):
+            load_copy(i, h).start()
 
     barrier = pltpu.get_barrier_semaphore()
     for j in range(1, sections):
@@ -152,10 +172,12 @@
         spread[k][me] = w_ref[me, flip(pos, masks[k], shards)]
 
     ahead = AHEAD
+    for j in range(shards - 1, 0, -1):
+        hidden_copy(j).start()
+    for h in range(heads):
+        turn(0, h)
     for k in range(min(ahead, shards)):
         start_spread(k)
-    for j in range(1, shards):
-        hidden_copy(j).start()
     feat[pos] = hidden_ref[:, columns]
 
     def collect(k):
@@ -185,6 +207,9 @@
         collect(k)
         if k + ahead < shards:
             start_spread(k + ahead)
+        if k < groups - 1:
+            for h in range(heads):
+                turn(k + 1, h)
         if k >= 1:
             forward(k - 1)
     forward(shards - 1)
@@ -209,12 +234,13 @@
         keep_copy(k).wait()
 
 
-AHEAD = 3
+AHEAD = 1
+LANES = 128
 
 
 def move(weights, hidden, source):
     sections, shards = lax.axis_size("section"), lax.axis_size("shard")
-    heads, _, piece, width = weights.shape
+    heads, piece, width = KVH, 2 * HD // shards, weights.shape[0]
     rows_in = hidden.shape[0]
     row_block = ROWS * heads // shards
     vmem = pl.BlockSpec(memory_space=pltpu.VMEM)
@@ -225,7 +251,7 @@
             jax.ShapeDtypeStruct((heads, piece, shards * width), jnp.bfloat16),
             jax.ShapeDtypeStruct((row_block, 2 * HD), jnp.bfloat16),
         ),
-        in_specs=[pl.BlockSpec(memory_space=pltpu.SMEM), vmem, vmem],
+        in_specs=[pl.BlockSpec(memory_space=pltpu.SMEM), pl.BlockSpec(memory_space=pl.ANY), vmem],
         out_specs=(pl.BlockSpec(memory_space=pl.ANY), vmem),
         scratch_shapes=[pltpu.VMEM((sections, piece, width), jnp.bfloat16)] * shards + [
             pltpu.VMEM((shards, sections, piece, width), jnp.bfloat16),
@@ -238,6 +264,9 @@
             dma((shards, sections)), dma((shards, sections)),
             dma((shards,)), dma((shards,)), dma((shards,)), dma((shards,)), dma((shards,)), dma((shards,)),
             dma(()),
+            pltpu.VMEM((heads, shards, piece, width), jnp.bfloat16),
+            pltpu.VMEM((shards * piece // LANES, heads, width, LANES), jnp.float32),
+            dma((shards * piece // LANES, heads)),
         ],
         compiler_params=pltpu.CompilerParams(
             collective_id=0, has_side_effects=True, vmem_limit_bytes=40 * 2**20),
@@ -286,11 +315,8 @@
     shards = lax.axis_size("shard")
     per_head = shards // KVH
     row_block = ROWS // per_head
-    piece = 2 * HD // shards
     source = jnp.argsort(section_to_group).astype(jnp.int32)
-    flipped = train_weights[0].astype(jnp.bfloat16).T
-    weights = flipped.reshape(KVH, shards, piece, flipped.shape[1])
-    kept, fresh = move(weights, hidden, source)
+    kept, fresh = move(train_weights[0], hidden, source)
     block = lax.axis_index("shard") % per_head
     row_lengths = lax.dynamic_slice_in_dim(lengths, block * row_block, row_block, 0)
     context = attend_rows(queries, kv_cache, fresh, row_lengths)
@@ -301,7 +327,7 @@
     sections, shards = mesh.shape["section"], mesh.shape["shard"]
     chunked = (
         sections == KVH and shards % KVH == 0 and shards & (shards - 1) == 0
-        and (2 * HD // shards) % 16 == 0 and (ROWS // shards) % 16 == 0
+        and (2 * HD // shards) % 16 == 0 and LANES % (2 * HD // shards) == 0 and (ROWS // shards) % 16 == 0
     )
     body = chunk_body if chunked else plain_body
     return jax.shard_map(

time: 180 us -> 164 us (0.911)
  Pallas kernels: 152 us -> 146 us
  other arithmetic: 6.81 us -> 1.4 us
  local copies, waits for them, and re-layouts: 19.9 us -> 15.5 us
    transpose x1 -> x0, local copies, waits for them, and re-layouts: 6.57 us -> none  [chunk_body(): flipped = train_weights[0].astype(jnp.bfloat16).T]
    transpose x1 -> x0, other arithmetic: 6.06 us -> none  [chunk_body(): flipped = train_weights[0].astype(jnp.bfloat16).T]
    pallas_call x1, Pallas kernels: 144 us -> 138 us  [move(): pl.pallas_call(functools.partial(move_kernel, sections, shards), out_shap...]
    unnamed x13 -> x11, local copies, waits for them, and re-layouts: 11.2 us -> 13.4 us
where the time goes in v2:
time: 164 us
  Pallas kernels  146 us (89%)
  local copies, waits for them, and re-layouts  15.5 us (9%)
    pallas_call x1, Pallas kernels, move(): pl.pallas_call(functools.partial(move_kernel, sections, shards), out_shap...  138 us
    unnamed x11, local copies, waits for them, and re-layouts  13.4 us
    pallas_call x1, Pallas kernels, attend_rows(): pl.pallas_call(attend_kernel, grid=(entries // step,), out_shape=jax.Shap...  7.71 us

profile of v2, /device:TPU:0, one launch (start us, length us, event | category | flops | bytes accessed | tf_op | source)
XLA Modules:
  0.0 163.8 jit_solution(5838505621181611261)
XLA Ops:
  0.6 0.7 dynamic_slice.3
  1.4 0.7 broadcast_in_dim.4.length_ref
  2.1 1.4 sort.17
  3.5 0.0 copy-start
  3.5 3.4 %copy-done = f32[1,2048,1024]{2,1,0:T(8,128)S(1)} copy-done((f32[1,2048,1024]{2,1,0:T(8,128)S(1)}, f32[1,2048,1024]{2,1,0:T(8,128)}, u32[]{:S(2)}) %copy-start) | copy-done | bytes 8388632
  6.9 0.0 copy-start.2
  6.9 1.0 copy-done.2
  7.9 0.0 copy-start.3
  7.9 138.5 %shard_map.77 = (bf16[4,32,16384]{2,1,0:T(8,128)(2,1)S(1)}, bf16[64,256]{1,0:T(8,128)(2,1)S(1)}) custom-call(s32[4]{0:T(128)S(1)} %get-tuple-element.5.source_ref, f32[2048,1024]{1,0:T(8,128)S(1)} %bitcast.9, bf16[16,16384]{1,0:T(8,128)(2,1)S(1)} %copy-done.2), custom_call_target="tpu_custom_call" | custom-call | flops 536870912 | bytes 8388608 | tf_op jit(solution)/shard_map/pallas_call | solution.py:248
  146.4 0.0 copy-start.1
  146.4 1.9 %copy-done.1 = bf16[4,32,16384]{2,1,0:T(8,128)(2,1)} copy-done((bf16[4,32,16384]{2,1,0:T(8,128)(2,1)}, bf16[4,32,16384]{2,1,0:T(8,128)(2,1)S(1)}, u32[]{:S(2)}) %copy-start.1) | copy-done | bytes 4194328
  148.4 0.7 copy.8.fresh_ref
  149.0 0.0 copy-done.3
  149.0 0.7 copy.9
  149.8 7.7 %shard_map.78 = bf16[64,16,128]{2,1,0:T(8,128)(2,1)} custom-call(bf16[64,16,128]{2,1,0:T(8,128)(2,1)} %bitcast.13, bf16[64,128,256]{2,1,0:T(8,128)(2,1)} %cache_ref.1, bf16[64,1,256]{2,1,0:T(2,128)(2,1)} %copy.8.fresh_ref, s32[64,1,128]{2,1,0:T(1,128)} %broadcast_in_dim.4.length_ref), custom_call_target="tpu_custom_call" | custom-call | tf_op jit(solution)/shard_map/pallas_call | solution.py:305
  157.5 1.7 %copy.12 = bf16[8,8,16,128]{3,1,2,0:T(8,128)(2,1)} copy(bf16[8,8,16,128]{3,2,1,0:T(8,128)(2,1)} %bitcast.12) | data formatting | bytes 524288
  159.2 4.6 %copy.14 = bf16[1,4,32,16384]{3,2,1,0:T(8,128)(2,1)} copy(bf16[1,4,32,16384]{3,2,1,0:T(8,128)(2,1)} %bitcast.10) | data formatting | bytes 8388608
  (1 shorter events, 0.0 us)
Async XLA Ops:
  3.5 3.4 %copy-start = (f32[1,2048,1024]{2,1,0:T(8,128)S(1)}, f32[1,2048,1024]{2,1,0:T(8,128)}, u32[]{:S(2)}) copy-start(f32[1,2048,1024]{2,1,0:T(8,128)} %param.6) | copy-start | bytes 25165828
  6.9 1.0 copy-start.2
  7.9 141.1 %copy-start.3 = (bf16[64,2048]{1,0:T(8,128)(2,1)S(1)}, bf16[64,2048]{1,0:T(8,128)(2,1)}, u32[]{:S(2)}) copy-start(bf16[64,2048]{1,0:T(8,128)(2,1)} %param.9) | copy-start | bytes 786436
  146.4 1.9 %copy-start.1 = (bf16[4,32,16384]{2,1,0:T(8,128)(2,1)}, bf16[4,32,16384]{2,1,0:T(8,128)(2,1)S(1)}, u32[]{:S(2)}) copy-start(bf16[4,32,16384]{2,1,0:T(8,128)(2,1)S(1)} %get-tuple-element.7) | copy-start | bytes 12582916

commit v3 on v2

--- a/solution.py
+++ b/solution.py
@@ -93,10 +93,10 @@
     return result
 
 
-def move_kernel(sections, shards, source_ref, train_ref, hidden_ref, out_ref, fresh_ref, *scratch):
+def move_kernel(sections, shards, source_ref, train_ref, hidden_ref, query_ref, cache_ref, length_ref, out_ref, context_ref, *scratch):
     spread = scratch[:shards]
     (stage, picked, feat, part, part_send, part_recv,
-     a_send, a_recv, b_send, b_recv, c_send, c_recv, h_send, h_recv, p_send, p_recv, local, w_ref, raw, raw_sem) = scratch[shards:]
+     a_send, a_recv, b_send, b_recv, c_send, c_recv, h_send, h_recv, p_send, p_recv, local, w_ref, raw, raw_sem, held, held_max, held_sum) = scratch[shards:]
     me = lax.axis_index("section")
     pos = lax.axis_index("shard")
     heads, _, piece, width = w_ref.shape
@@ -203,6 +203,34 @@
         for h in range(heads):
             part[h, pl.ds(pl.multiple_of(p * piece, piece), piece), :] = value[h * piece:(h + 1) * piece]
 
+    scale = 1.0 / math.sqrt(HD)
+    some = cache_ref.shape[0] // shards
+
+    def attend_cached(k):
+        rows = slice(k * some, (k + 1) * some)
+        cache = cache_ref[rows]
+        scores = lax.dot_general(query_ref[rows], cache[:, :, :HD], (((2,), (2,)), ((0,), (0,))),
+                                 preferred_element_type=jnp.float32) * scale
+        valid = lax.broadcasted_iota(jnp.int32, scores.shape, 2) < length_ref[rows]
+        scores = jnp.where(valid, scores, -1e30)
+        highest = jnp.max(scores, axis=-1, keepdims=True)
+        weights = jnp.where(valid, jnp.exp(scores - highest), 0.0)
+        held[rows] = lax.dot_general(weights.astype(jnp.bfloat16), cache[:, :, HD:], (((2,), (1,)), ((0,), (0,))),
+                                     preferred_element_type=jnp.float32)
+        held_max[rows] = jnp.broadcast_to(highest, scores.shape)
+        held_sum[rows] = jnp.broadcast_to(jnp.sum(weights, axis=-1, keepdims=True), scores.shape)
+
+    def attend_fresh(k, fresh):
+        rows = slice(k * some, (k + 1) * some)
+        key, value = fresh[rows, :HD][:, None, :], fresh[rows, HD:][:, None, :]
+        score = jnp.sum(query_ref[rows].astype(jnp.float32) * key, axis=-1, keepdims=True) * scale
+        highest = jnp.maximum(held_max[rows], score)
+        old = jnp.exp(held_max[rows] - highest)
+        new = jnp.exp(score - highest)
+        total = held_sum[rows] * old + new
+        prob = (new / total).astype(jnp.bfloat16).astype(jnp.float32)
+        context_ref[rows] = (held[rows] * (old / total) + prob * value).astype(context_ref.dtype)
+
     for k in range(shards):
         collect(k)
         if k + ahead < shards:
@@ -212,6 +240,7 @@
                 turn(k + 1, h)
         if k >= 1:
             forward(k - 1)
+        attend_cached(k)
     forward(shards - 1)
 
     for h in range(heads):
@@ -229,7 +258,9 @@
     for j in range(1, shards):
         part_copy(j).wait()
         total = total + part_recv[j]
-    fresh_ref[...] = total.astype(fresh_ref.dtype)
+    fresh = total.astype(jnp.bfloat16).astype(jnp.float32)
+    for k in range(shards):
+        attend_fresh(k, fresh)
     for k in range(shards):
         keep_copy(k).wait()
 
@@ -238,20 +269,22 @@
 LANES = 128
 
 
-def move(weights, hidden, source):
+def move(weights, hidden, source, queries, cache, row_lengths):
     sections, shards = lax.axis_size("section"), lax.axis_size("shard")
     heads, piece, width = KVH, 2 * HD // shards, weights.shape[0]
     rows_in = hidden.shape[0]
     row_block = ROWS * heads // shards
+    entries = cache.shape[0]
+    lengths = jnp.broadcast_to(row_lengths[:, None, None], (entries, 1, LEN))
     vmem = pl.BlockSpec(memory_space=pltpu.VMEM)
     dma = pltpu.SemaphoreType.DMA
     return pl.pallas_call(
         functools.partial(move_kernel, sections, shards),
         out_shape=(
             jax.ShapeDtypeStruct((heads, piece, shards * width), jnp.bfloat16),
-            jax.ShapeDtypeStruct((row_block, 2 * HD), jnp.bfloat16),
+            jax.ShapeDtypeStruct((entries, QPK, HD), jnp.bfloat16),
         ),
-        in_specs=[pl.BlockSpec(memory_space=pltpu.SMEM), pl.BlockSpec(memory_space=pl.ANY), vmem],
+        in_specs=[pl.BlockSpec(memory_space=pltpu.SMEM), pl.BlockSpec(memory_space=pl.ANY), vmem, vmem, vmem, vmem],
         out_specs=(pl.BlockSpec(memory_space=pl.ANY), vmem),
         scratch_shapes=[pltpu.VMEM((sections, piece, width), jnp.bfloat16)] * shards + [
             pltpu.VMEM((shards, sections, piece, width), jnp.bfloat16),
@@ -267,48 +300,11 @@
             pltpu.VMEM((heads, shards, piece, width), jnp.bfloat16),
             pltpu.VMEM((shards * piece // LANES, heads, width, LANES), jnp.float32),
             dma((shards * piece // LANES, heads)),
-        ],
+        ] + [pltpu.VMEM((entries, QPK, HD), jnp.float32)] * 3,
         compiler_params=pltpu.CompilerParams(
-            collective_id=0, has_side_effects=True, vmem_limit_bytes=40 * 2**20),
+            collective_id=0, has_side_effects=True, vmem_limit_bytes=50 * 2**20),
         cost_estimate=pl.CostEstimate(flops=2 * ROWS * width * heads * piece * shards, bytes_accessed=4 * weights.size, transcendentals=0),
-    )(source, weights, hidden)
-
-
-def attend_kernel(query_ref, cache_ref, fresh_ref, length_ref, out_ref):
-    scale = 1.0 / math.sqrt(HD)
-    query = query_ref[...]
-    cache = cache_ref[...]
-    fresh = fresh_ref[...].astype(jnp.float32)
-    scores = lax.dot_general(query, cache[:, :, :HD], (((2,), (2,)), ((0,), (0,))),
-                             preferred_element_type=jnp.float32) * scale
-    slot = lax.broadcasted_iota(jnp.int32, scores.shape, 2)
-    valid = slot < length_ref[...]
-    scores = jnp.where(valid, scores, -1e30)
-    fresh_score = jnp.sum(query.astype(jnp.float32) * fresh[:, :, :HD], axis=-1, keepdims=True) * scale
-    highest = jnp.maximum(jnp.max(scores, axis=-1, keepdims=True), fresh_score)
-    weights = jnp.where(valid, jnp.exp(scores - highest), 0.0)
-    fresh_weight = jnp.exp(fresh_score - highest)
-    total = jnp.sum(weights, axis=-1, keepdims=True) + fresh_weight
-    probs = (weights / total).astype(jnp.bfloat16)
-    fresh_prob = (fresh_weight / total).astype(jnp.bfloat16).astype(jnp.float32)
-    context = lax.dot_general(probs, cache[:, :, HD:], (((2,), (1,)), ((0,), (0,))),
-                              preferred_element_type=jnp.float32)
-    context = context + fresh_prob * fresh[:, :, HD:]
-    out_ref[...] = context.astype(out_ref.dtype)
-
-
-def attend_rows(queries, cache, fresh, row_lengths):
-    entries = cache.shape[0]
-    step = 8
-    spec = lambda *tail: pl.BlockSpec((step,) + tail, lambda i: (i, 0, 0))
-    lengths = jnp.broadcast_to(row_lengths[:, None, None], (entries, 1, LEN))
-    return pl.pallas_call(
-        attend_kernel,
-        grid=(entries // step,),
-        out_shape=jax.ShapeDtypeStruct((entries, QPK, HD), jnp.bfloat16),
-        in_specs=[spec(QPK, HD), spec(LEN, 2 * HD), spec(1, 2 * HD), spec(1, LEN)],
-        out_specs=spec(QPK, HD),
-    )(queries.reshape(entries, QPK, HD), cache, fresh.reshape(entries, 1, 2 * HD), lengths).reshape(entries, QPK * HD)
+    )(source, weights, hidden, queries.reshape(entries, QPK, HD), cache, lengths)
 
 
 def chunk_body(train_weights, section_to_group, hidden, queries, kv_cache, lengths):
@@ -316,10 +312,10 @@
     per_head = shards // KVH
     row_block = ROWS // per_head
     source = jnp.argsort(section_to_group).astype(jnp.int32)
-    kept, fresh = move(train_weights[0], hidden, source)
     block = lax.axis_index("shard") % per_head
     row_lengths = lax.dynamic_slice_in_dim(lengths, block * row_block, row_block, 0)
-    context = attend_rows(queries, kv_cache, fresh, row_lengths)
+    kept, context = move(train_weights[0], hidden, source, queries, kv_cache, row_lengths)
+    context = context.reshape(queries.shape)
     return (context, kept[None])
 
 

time: 164 us -> 150 us (0.915)
  local copies, waits for them, and re-layouts: 15.5 us -> 8.23 us
  Pallas kernels: 146 us -> 140 us
    pallas_call x1 -> x0, Pallas kernels: 7.71 us -> none  [attend_rows(): pl.pallas_call(attend_kernel, grid=(entries // step,), out_shape=jax.Shap...]
    unnamed x11 -> x5, local copies, waits for them, and re-layouts: 13.4 us -> 7.37 us
where the time goes in v3:
time: 150 us
  Pallas kernels  140 us (93%)
  local copies, waits for them, and re-layouts  8.23 us (5%)
    pallas_call x1, Pallas kernels, move(): pl.pallas_call(functools.partial(move_kernel, sections, shards), out_shap...  140 us
    unnamed x5, local copies, waits for them, and re-layouts  7.37 us

profile of v3, /device:TPU:0, one launch (start us, length us, event | category | flops | bytes accessed | tf_op | source)
XLA Modules:
  0.0 150.2 jit_solution(9666478491850008506)
XLA Ops:
  0.6 0.7 dynamic_slice.3
  1.4 1.4 sort.17
  2.8 0.1 broadcast_in_dim.4.length_ref
  2.9 1.0 copy.8
  3.9 0.0 copy-start
  3.9 1.0 copy-done
  5.0 139.9 %shard_map.77 = (bf16[4,32,16384]{2,1,0:T(8,128)(2,1)}, bf16[64,16,128]{2,1,0:T(8,128)(2,1)S(1)}) custom-call(s32[4]{0:T(128)S(1)} %get-tuple-element.5.source_ref, f32[2048,1024]{1,0:T(8,128)} %bitcast.10, bf16[16,16384]{1,0:T(8,128)(2,1)S(1)} %copy-done, bf16[64,16,128]{2,1,0:T(8,128)(2,1)S(1)} %bitcast.8, bf16[64,128,256]{2,1,0:T(8,128)(2,1)} %cache_ref.1, ...), custom_call_target="tpu_custom_call" | custom-call | flops 536870912 | bytes 8388608 | tf_op jit(solution)/shard_map/pallas_call | solution.py:281
  144.8 0.8 copy.11
  145.6 4.6 %copy.13 = bf16[1,4,32,16384]{3,2,1,0:T(8,128)(2,1)} copy(bf16[1,4,32,16384]{3,2,1,0:T(8,128)(2,1)} %bitcast.11) | data formatting | bytes 8388608
  (1 shorter events, 0.0 us)
Async XLA Ops:
  3.9 1.0 copy-start

commit v4 on v3

--- a/solution.py
+++ b/solution.py
@@ -193,6 +193,8 @@
         for copy in collect_copies(k):
             copy.wait()
         keep_copy(k).start()
+
+    def multiply(k):
         if k == 0:
             for j in range(1, shards):
                 hidden_copy(j).wait()
@@ -232,6 +234,8 @@
         context_ref[rows] = (held[rows] * (old / total) + prob * value).astype(context_ref.dtype)
 
     for k in range(shards):
+        if k >= 1:
+            forward(k - 1)
         collect(k)
         if k + ahead < shards:
             start_spread(k + ahead)
@@ -239,9 +243,10 @@
             for h in range(heads):
                 turn(k + 1, h)
         if k >= 1:
-            forward(k - 1)
+            multiply(k - 1)
         attend_cached(k)
     forward(shards - 1)
+    multiply(shards - 1)
 
     for h in range(heads):
         turned = part[h].T

time: 150 us -> 145 us (0.967)
  Pallas kernels: 140 us -> 134 us
    pallas_call x1, Pallas kernels: 140 us -> 134 us  [move(): pl.pallas_call(functools.partial(move_kernel, sections, shards), out_shap...]
where the time goes in v4:
time: 145 us; the launch traced here: 144 us
  Pallas kernels  134 us (92%)
  local copies, waits for them, and re-layouts  8.23 us (6%)
    pallas_call x1, Pallas kernels, move(): pl.pallas_call(functools.partial(move_kernel, sections, shards), out_shap...  134 us
    unnamed x5, local copies, waits for them, and re-layouts  7.37 us

profile of v4, /device:TPU:0, one launch (start us, length us, event | category | flops | bytes accessed | tf_op | source)
XLA Modules:
  0.0 144.3 jit_solution(11721177456935287837)
XLA Ops:
  0.6 0.7 dynamic_slice.3
  1.4 1.4 sort.17
  2.8 0.1 broadcast_in_dim.4.length_ref
  2.9 1.0 copy.8
  3.9 0.0 copy-start
  3.9 1.0 copy-done
  5.0 134.0 %shard_map.77 = (bf16[4,32,16384]{2,1,0:T(8,128)(2,1)}, bf16[64,16,128]{2,1,0:T(8,128)(2,1)S(1)}) custom-call(s32[4]{0:T(128)S(1)} %get-tuple-element.5.source_ref, f32[2048,1024]{1,0:T(8,128)} %bitcast.10, bf16[16,16384]{1,0:T(8,128)(2,1)S(1)} %copy-done, bf16[64,16,128]{2,1,0:T(8,128)(2,1)S(1)} %bitcast.8, bf16[64,128,256]{2,1,0:T(8,128)(2,1)} %cache_ref.1, ...), custom_call_target="tpu_custom_call" | custom-call | flops 536870912 | bytes 8388608 | tf_op jit(solution)/shard_map/pallas_call | solution.py:286
  139.0 0.8 copy.11
  139.7 4.6 %copy.13 = bf16[1,4,32,16384]{3,2,1,0:T(8,128)(2,1)} copy(bf16[1,4,32,16384]{3,2,1,0:T(8,128)(2,1)} %bitcast.11) | data formatting | bytes 8388608
  (1 shorter events, 0.0 us)
Async XLA Ops:
  3.9 1.0 copy-start
